TPU v7x, 32 devices: a whole 2x2x4 slice. The times are simulated.
32 devices in a mesh: replica: 4 (over z), shard: 8 (over y, x, core).
Axes of the slice: x: 2, y: 2, z: 4, core: 2. Of those that a mesh axis runs over, the one named last changes fastest.
Arguments:
- grads: bfloat16 [4, 2048, 6144], P('replica', 'shard'), may hold values from -3 to 3
- owner_map: int32 [4, 12], replicated, may hold values from 0 to 23, as said below
- factor_left: float32 [32, 3, 512, 512], P(('replica', 'shard')), may hold values from -1 to 7
- factor_right: float32 [32, 3, 512, 512], P(('replica', 'shard')), may hold values from -1 to 7
- left_inverse_roots: bfloat16 [32, 3, 512, 512], P(('replica', 'shard')), may hold values from -1 to 7
- right_inverse_roots: bfloat16 [32, 3, 512, 512], P(('replica', 'shard')), may hold values from -1 to 7
Outputs:
- new_left: float32 [32, 3, 512, 512], P(('replica', 'shard'))
- new_right: float32 [32, 3, 512, 512], P(('replica', 'shard'))
- update: bfloat16 [2048, 6144], P('shard')
Inputs may be any that keep to these rules, and one draw needn't show every extreme that they name: `owner_map`: within one block row and one replica's 3 block columns no two blocks name the same owner; within one replica's 3 block columns no two blocks share an entry; some owner holds 3 blocks in every draw.
All inputs are finite; a program needn't handle non-finite values.
Results may differ from a plain program's by a relative error of at most 0.0058.
Values may be sent and summed in bfloat16 or wider, within the bound.
A program may use at most 128 MiB of HBM per device.

v0:
```python
import jax
import jax.numpy as jnp
from jax import lax
from jax.sharding import PartitionSpec as P


def precondition(
    row_blocks, slot_rows, factor_left, factor_right, left_inverse_roots, right_inverse_roots
):
    block_size = row_blocks.shape[1]
    collected_blocks = jnp.einsum(
        "ti,iab->tab", slot_rows, row_blocks, preferred_element_type=jnp.float32
    ).astype(jnp.bfloat16)
    left_gram_matrix = jnp.einsum(
        "zqw,zfw->zqf", collected_blocks, collected_blocks, preferred_element_type=jnp.float32
    )
    right_gram_matrix = jnp.einsum(
        "iyj,iyv->ijv", collected_blocks, collected_blocks, preferred_element_type=jnp.float32
    )
    new_left = 0.9 * factor_left[0] + 0.1 / block_size * left_gram_matrix
    new_right = 0.9 * factor_right[0] + 0.1 / block_size * right_gram_matrix
    preconditioned_update = jnp.einsum(
        "ivp,ips->ivs", left_inverse_roots[0], collected_blocks, preferred_element_type=jnp.float32
    ).astype(jnp.bfloat16)
    product = jnp.einsum(
        "ivp,ips->ivs",
        preconditioned_update,
        right_inverse_roots[0],
        preferred_element_type=jnp.float32,
    ).astype(jnp.bfloat16)
    by_rows = jnp.einsum(
        "ti,tab->iab", slot_rows, product, preferred_element_type=jnp.float32
    ).astype(jnp.bfloat16)
    return (new_left[None], new_right[None], by_rows)


def body(grads, owner_map, factor_left, factor_right, left_inverse_roots, right_inverse_roots):
    num_replicas = lax.axis_size("replica")
    num_shards = lax.axis_size("shard")
    replica_at = lax.axis_index("replica")
    shard_at = lax.axis_index("shard")
    strip_rows = grads.shape[1]
    columns = grads.shape[2]
    capacity = factor_left.shape[1]
    block_size = factor_left.shape[2]
    block_rows = owner_map.shape[0]
    block_cols = owner_map.shape[1]
    per_group = block_cols // num_replicas
    row_index = shard_at * strip_rows // block_size
    row_entries = lax.dynamic_index_in_dim(owner_map, row_index, 0, keepdims=False)
    group_entries = lax.dynamic_slice_in_dim(owner_map, replica_at * per_group, per_group, 1)
    targets = shard_at * capacity + jnp.arange(capacity, dtype=jnp.int32)
    slot_rows = jnp.sum(
        (group_entries[None, :, :] == targets[:, None, None]).astype(jnp.float32), axis=2
    ).astype(jnp.bfloat16)
    pieces = grads[0].reshape(strip_rows, block_cols, block_size).transpose(1, 0, 2)
    column_ids = jnp.arange(block_cols, dtype=jnp.int32)
    owner_dev = column_ids // per_group * num_shards + row_entries // capacity
    device_ids = jnp.arange(num_replicas * num_shards, dtype=jnp.int32)
    destination = (owner_dev[None, :] == device_ids[:, None]).astype(jnp.bfloat16)
    outgoing = jnp.einsum(
        "dk,kab->dab", destination, pieces, preferred_element_type=jnp.float32
    ).astype(jnp.bfloat16)
    incoming = lax.all_to_all(
        outgoing, ("replica", "shard"), split_axis=0, concat_axis=0, tiled=True
    )
    summed = jnp.sum(
        incoming.reshape(num_replicas, num_shards, strip_rows, block_size),
        axis=0,
        dtype=jnp.float32,
    )
    row_blocks = summed.astype(jnp.bfloat16).reshape(block_rows, block_size, block_size)
    new_left, new_right, by_rows = precondition(
        row_blocks, slot_rows, factor_left, factor_right, left_inverse_roots, right_inverse_roots
    )
    tiled = jnp.broadcast_to(
        by_rows.reshape(1, num_shards, strip_rows, block_size),
        (num_replicas, num_shards, strip_rows, block_size),
    )
    returned = lax.all_to_all(
        tiled.reshape(num_replicas * num_shards, strip_rows, block_size),
        ("replica", "shard"),
        split_axis=0,
        concat_axis=0,
        tiled=True,
    )
    own_pieces = jnp.einsum(
        "dk,dab->kab", destination, returned, preferred_element_type=jnp.float32
    ).astype(jnp.bfloat16)
    update = own_pieces.transpose(1, 0, 2).reshape(strip_rows, columns)
    return (new_left, new_right, update)


def solution(mesh):
    in_specs = (
        P("replica", "shard", None),
        P(),
        P(("replica", "shard"), None, None, None),
        P(("replica", "shard"), None, None, None),
        P(("replica", "shard"), None, None, None),
        P(("replica", "shard"), None, None, None),
    )
    out_specs = (
        P(("replica", "shard"), None, None, None),
        P(("replica", "shard"), None, None, None),
        P("shard", None),
    )
    return jax.shard_map(body, mesh=mesh, in_specs=in_specs, out_specs=out_specs, check_vma=False)
```

profile of v0, /device:TPU:0, one launch (start us, length us, event | category | flops | bytes accessed | tf_op | source)
XLA Modules:
  0.0 463.5 jit_solution(14554464955706810524)
XLA Ops:
  0.6 0.0 copy-start
  0.7 4.7 %copy.62 = bf16[1,256,6144]{1,2,0:T(8,128)(2,1)} copy(bf16[1,256,6144]{2,1,0:T(8,128)(2,1)} %param.6) | data formatting | bytes 6291456 | tf_op args[0]
  5.4 0.0 copy-start.4
  5.4 7.7 %copy.63 = bf16[12,256,512]{2,0,1:T(8,128)(2,1)} copy(bf16[12,256,512]{1,2,0:T(8,128)(2,1)} %bitcast.45) | data formatting | bytes 6291456 | tf_op jit(solution)/shard_map/transpose | solution.py:56
  13.1 0.0 copy-done.4
  13.1 7.8 %convolution_convert_fusion = bf16[32,256,512]{2,0,1:T(8,128)(2,1)} fusion(bf16[12,256,512]{2,0,1:T(8,128)(2,1)} %copy.63, s32[12]{0:T(128)S(1)} %fusion.26), kind=kOutput, calls=%fused_computation.2 | convolution fusion | flops 104857984 | bytes 11534384 | tf_op jit(solution)/shard_map/dk,kab->dab/dot_general | solution.py:61
  21.0 11.3 %copy.64 = bf16[32,256,512]{2,1,0:T(8,128)(2,1)} copy(bf16[32,256,512]{2,0,1:T(8,128)(2,1)} %convolution_convert_fusion) | data formatting | bytes 16777216 | tf_op jit(solution)/shard_map/convert_element_type | solution.py:63
  32.3 7.6 %all-to-all-start = ((bf16[32,256,512]{2,1,0:T(8,128)(2,1)}), bf16[32,256,512]{2,1,0:T(8,128)(2,1)}, u32[]{:S(2)}, u32[]{:S(2)}) async-start(bf16[32,256,512]{2,1,0:T(8,128)(2,1)} %copy.64), calls=%async_computation | async-start | bytes 16777216 | tf_op jit(solution)/shard_map/all_to_all | solution.py:64
  40.0 0.1 constant_dynamic-slice_fusion
  40.0 0.2 convert_reduce_fusion
  40.2 185.7 %all-to-all-done = bf16[32,256,512]{2,1,0:T(8,128)(2,1)} async-done(((bf16[32,256,512]{2,1,0:T(8,128)(2,1)}), bf16[32,256,512]{2,1,0:T(8,128)(2,1)}, u32[]{:S(2)}, u32[]{:S(2)}) %all-to-all-start) | async-done | bytes 8388640 | tf_op jit(solution)/shard_map/all_to_all | solution.py:64
  225.9 6.7 %reduce_sum.22 = bf16[8,256,512]{2,1,0:T(8,128)(2,1)} reduce(bf16[4,8,256,512]{3,2,1,0:T(8,128)(2,1)} %bitcast.6, bf16[]{:T(256)} %constant.53.clone.1), dimensions={0}, to_apply=%region_1.2 | reduce | flops 3145728 | bytes 10485762 | tf_op jit(solution)/shard_map/reduce_sum | solution.py:67
  232.6 0.0 copy-start.5
  232.6 4.7 %fusion.8 = bf16[3,512,512]{2,0,1:T(4,128)(2,1)} fusion(bf16[4,512,512]{2,1,0:T(8,128)(2,1)} %bitcast.47, bf16[3,4]{1,0:T(4,128)(2,1)S(1)} %convert_reduce_fusion), kind=kOutput, calls=%fused_computation.11 | convolution fusion | flops 6291456 | bytes 3670040 | tf_op jit(solution)/shard_map/ti,iab->tab/dot_general | solution.py:11
  237.3 0.0 copy-done
  237.3 0.0 copy-done.5
  237.3 4.9 %convolution_convert_fusion.1 = bf16[3,512,512]{2,1,0:T(8,128)(2,1)} fusion(bf16[1,3,512,512]{3,2,1,0:T(8,128)(2,1)S(1)} %copy-done, bf16[1,3,512,512]{3,2,1,0:T(8,128)(2,1)S(1)} %copy-done.5, bf16[3,512,512]{2,0,1:T(4,128)(2,1)} %fusion.8), kind=kOutput, calls=%fused_computation.14 | convolution fusion | flops 1612185600 | bytes 6291456 | tf_op jit(solution)/shard_map/ivp,ips->ivs/dot_general | solution.py:25
  242.2 3.5 fusion.10
  245.7 0.4 copy.74
  246.1 4.2 broadcast_in_dim.20
  250.3 3.9 all-to-all-start.1
  254.2 0.0 copy-start.2
  254.2 0.0 copy-start.3
  254.2 6.5 %fusion.2 = f32[1,3,512,512]{3,2,1,0:T(8,128)} fusion(f32[1,3,512,512]{3,2,1,0:T(8,128)} %param.9, bf16[3,512,512]{2,0,1:T(4,128)(2,1)} %fusion.8), kind=kOutput, calls=%fused_computation.5 | convolution fusion | flops 807665664 | bytes 7864320 | tf_op jit(solution)/shard_map/iyj,iyv->ijv/dot_general | solution.py:17
  260.7 0.0 copy-done.2
  260.7 0.0 copy-done.3
  260.7 3.0 fusion.3
  263.8 176.5 %all-to-all-done.1 = bf16[32,256,512]{2,1,0:T(8,128)(2,1)} async-done(((bf16[32,256,512]{2,1,0:T(8,128)(2,1)}), bf16[32,256,512]{2,1,0:T(8,128)(2,1)}, u32[]{:S(2)}, u32[]{:S(2)}) %all-to-all-start.1) | async-done | bytes 8388640 | tf_op jit(solution)/shard_map/all_to_all | solution.py:80
  440.3 11.0 %convert_bitcast_fusion = bf16[256,12,512]{2,1,0:T(8,128)(2,1)} fusion(bf16[32,256,512]{2,1,0:T(8,128)(2,1)} %all-to-all-done.1, s32[12]{0:T(128)S(1)} %fusion.26), kind=kOutput, calls=%fused_computation.3 | convolution fusion | flops 102236544 | bytes 11534384 | tf_op jit(solution)/shard_map/dk,dab->kab/dot_general | solution.py:87
  451.3 7.5 %copy.76 = bf16[256,12,512]{0,2,1:T(8,128)(2,1)} copy(bf16[256,12,512]{2,1,0:T(8,128)(2,1)} %convert_bitcast_fusion) | data formatting | bytes 6291456 | tf_op jit(solution)/shard_map/convert_element_type | solution.py:89
  458.8 4.7 %copy.77 = bf16[256,6144]{1,0:T(8,128)(2,1)} copy(bf16[256,6144]{0,1:T(8,128)(2,1)} %bitcast.44) | data formatting | bytes 6291456
  463.5 0.0 copy-done.1
  (3 shorter events, 0.0 us)
Async XLA Ops:
  0.6 236.7 %copy-start = (bf16[1,3,512,512]{3,2,1,0:T(8,128)(2,1)S(1)}, bf16[1,3,512,512]{3,2,1,0:T(8,128)(2,1)}, u32[]{:S(2)}) copy-start(bf16[1,3,512,512]{3,2,1,0:T(8,128)(2,1)} %param.11) | copy-start | bytes 4718596
  5.4 7.7 %copy-start.4 = (s32[4,12]{1,0:T(4,128)S(1)}, s32[4,12]{1,0:T(4,128)}, u32[]{:S(2)}) copy-start(s32[4,12]{1,0:T(4,128)} %param.7) | copy-start | bytes 580
  32.3 193.6 %all-to-all-start = ((bf16[32,256,512]{2,1,0:T(8,128)(2,1)}), bf16[32,256,512]{2,1,0:T(8,128)(2,1)}, u32[]{:S(2)}, u32[]{:S(2)}) async-start(bf16[32,256,512]{2,1,0:T(8,128)(2,1)} %copy.64), calls=%async_computation | async-start | bytes 16777216 | tf_op jit(solution)/shard_map/all_to_all | solution.py:64
  232.6 4.7 %copy-start.5 = (bf16[1,3,512,512]{3,2,1,0:T(8,128)(2,1)S(1)}, bf16[1,3,512,512]{3,2,1,0:T(8,128)(2,1)}, u32[]{:S(2)}) copy-start(bf16[1,3,512,512]{3,2,1,0:T(8,128)(2,1)} %param.10) | copy-start | bytes 4718596
  250.3 190.0 %all-to-all-start.1 = ((bf16[32,256,512]{2,1,0:T(8,128)(2,1)}), bf16[32,256,512]{2,1,0:T(8,128)(2,1)}, u32[]{:S(2)}, u32[]{:S(2)}) async-start(bf16[32,256,512]{2,1,0:T(8,128)(2,1)} %bitcast.43), calls=%async_computation.1 | async-start | bytes 16777216 | tf_op jit(solution)/shard_map/all_to_all | solution.py:80
  254.2 6.6 %copy-start.2 = (bf16[3,512,512]{2,0,1:T(4,128)(2,1)S(1)}, bf16[3,512,512]{2,0,1:T(4,128)(2,1)}, u32[]{:S(2)}) copy-start(bf16[3,512,512]{2,0,1:T(4,128)(2,1)} %fusion.8) | copy-start | bytes 4718596
  254.2 6.5 %copy-start.3 = (f32[1,3,512,512]{3,2,1,0:T(8,128)S(1)}, f32[1,3,512,512]{3,2,1,0:T(8,128)}, u32[]{:S(2)}) copy-start(f32[1,3,512,512]{3,2,1,0:T(8,128)} %param.8) | copy-start | bytes 9437188
  458.8 4.8 %copy-start.1 = (bf16[1,3,512,512]{3,2,1,0:T(8,128)(2,1)S(1)}, bf16[1,3,512,512]{3,2,1,0:T(8,128)(2,1)}, u32[]{:S(2)}) copy-start(bf16[1,3,512,512]{3,2,1,0:T(8,128)(2,1)} %param.11) | copy-start | bytes 4718596
where the time goes:
time: 464 us
  waiting for transfers between devices  362 us (78%)
  matrix products  41.5 us (9%)
  local copies, waits for them, and re-layouts  40.7 us (9%)
  starting transfers between devices  11.5 us (2%)
  other arithmetic  6.87 us (1%)
    all_to_all x1, waiting for transfers between devices, body(): lax.all_to_all(outgoing, ('replica', 'shard'), split_axis=0, concat_axis=...  186 us
    all_to_all x1, waiting for transfers between devices, body(): lax.all_to_all(tiled.reshape(num_replicas * num_shards, strip_rows, block...  177 us
    convert_element_type x1, local copies, waits for them, and re-layouts, body(): outgoing = jnp.einsum('dk,kab->dab', destination, pieces, preferred_eleme...  11.3 us
    dot_general x1, matrix products, body(): jnp.einsum('dk,dab->kab', destination, returned, preferred_element_type=j...  11 us
    unnamed x14, local copies, waits for them, and re-layouts  9.53 us
  transfers between devices with their start and end apart: 2, of which 2 were waited for; matrix products, arithmetic and copies ran while one was open for 2% of the time, Pallas kernels for 0%

commit v1 on v0

v1 whole, which is shorter than its diff:
```python
import jax
import jax.numpy as jnp
from jax import lax
from jax.sharding import PartitionSpec as P


def body(grads, owner_map, factor_left, factor_right, left_roots, right_roots):
    replicas = lax.axis_size("replica")
    shards = lax.axis_size("shard")
    replica_at = lax.axis_index("replica")
    shard_at = lax.axis_index("shard")
    strip_rows, columns = grads.shape[1:]
    capacity, block_size = factor_left.shape[1:3]
    block_rows, block_cols = owner_map.shape
    per_group = block_cols // replicas
    group_entries = lax.dynamic_slice_in_dim(owner_map, replica_at * per_group, per_group, 1)
    row_entries = lax.dynamic_index_in_dim(
        group_entries, shard_at * strip_rows // block_size, 0, keepdims=False
    )
    parts = grads[0].reshape(strip_rows, replicas, per_group, block_size).transpose(1, 2, 0, 3)
    copies = lax.all_to_all(parts, "replica", split_axis=0, concat_axis=0, tiled=True)
    pieces = jnp.sum(copies, axis=0, dtype=jnp.float32).astype(jnp.bfloat16)
    owners = row_entries // capacity
    to_owner = owners[None, :] == jnp.arange(shards, dtype=jnp.int32)[:, None]
    to_owner = to_owner.astype(jnp.bfloat16)
    outgoing = jnp.einsum("dk,kab->dab", to_owner, pieces)
    incoming = lax.all_to_all(outgoing, "shard", split_axis=0, concat_axis=0, tiled=True)
    row_blocks = incoming.reshape(block_rows, block_size, block_size)
    targets = shard_at * capacity + jnp.arange(capacity, dtype=jnp.int32)
    slot_rows = jnp.any(group_entries[None] == targets[:, None, None], axis=2).astype(jnp.bfloat16)
    g = jnp.einsum("ti,iab->tab", slot_rows, row_blocks)
    f32 = dict(preferred_element_type=jnp.float32)
    left_gram = jnp.einsum("tab,tcb->tac", g, g, **f32)
    right_gram = jnp.einsum("tab,tac->tbc", g, g, **f32)
    new_left = 0.9 * factor_left[0] + 0.1 / block_size * left_gram
    new_right = 0.9 * factor_right[0] + 0.1 / block_size * right_gram
    applied = jnp.einsum("tab,tbc->tac", left_roots[0], g, **f32).astype(jnp.bfloat16)
    product = jnp.einsum("tab,tbc->tac", applied, right_roots[0], **f32).astype(jnp.bfloat16)
    by_rows = jnp.einsum("ti,tab->iab", slot_rows, product)
    by_rows = by_rows.reshape(shards, strip_rows, block_size)
    returned = lax.all_to_all(by_rows, "shard", split_axis=0, concat_axis=0, tiled=True)
    own = jnp.einsum("dk,dab->akb", to_owner, returned).reshape(strip_rows, per_group * block_size)
    update = lax.all_gather(own, "replica", axis=1, tiled=True)
    return new_left[None], new_right[None], update


def solution(mesh):
    owned = P(("replica", "shard"), None, None, None)
    in_specs = (P("replica", "shard", None), P(), owned, owned, owned, owned)
    out_specs = (owned, owned, P("shard", None))
    return jax.shard_map(body, mesh=mesh, in_specs=in_specs, out_specs=out_specs, check_vma=False)
```

time: 464 us -> 249 us (0.54)
  waiting for transfers between devices: 362 us -> 149 us
  blocking collectives: 0 us -> 29 us
  local copies, waits for them, and re-layouts: 40.7 us -> 18 us
  matrix products: 41.5 us -> 25.3 us
  between operations: 0.73 us -> 14.1 us
    all_to_all x2, waiting for transfers between devices: 362 us -> 97 us  [the longest x1 70.7 us: body(): lax.all_to_all(parts, 'replica', split_axis=0, concat_axis=0, tiled=True)]
    all_gather x0 -> x1, waiting for transfers between devices: none -> 51.7 us  [body(): update = lax.all_gather(own, 'replica', axis=1, tiled=True)]
    all_to_all x0 -> x1, blocking collectives: none -> 29 us  [body(): lax.all_to_all(by_rows, 'shard', split_axis=0, concat_axis=0, tiled=True)]
    convert_element_type x3 -> x0, local copies, waits for them, and re-layouts: 19.2 us -> none  [the longest x1 11.3 us: body(): outgoing = jnp.einsum('dk,kab->dab', destination, pieces, preferred_eleme...]
    dot_general x7, matrix products: 41.5 us -> 25.3 us  [the longest x1 6.34 us: body(): left_gram = jnp.einsum('tab,tcb->tac', g, g, **f32)]
    transpose x1, local copies, waits for them, and re-layouts: 7.71 us -> 2.29 us  [body(): jnp.einsum('dk,dab->akb', to_owner, returned)]
    dot_general x0 -> x3, local copies, waits for them, and re-layouts: none -> 5.27 us  [the longest x1 2.86 us: body(): g = jnp.einsum('ti,iab->tab', slot_rows, row_blocks)]
    unnamed x14 -> x10, local copies, waits for them, and re-layouts: 9.53 us -> 9.41 us
  transfers between devices with their start and end apart: 2 -> 3, of which waited for: 2 -> 3; matrix products, arithmetic and copies ran while one was open for 2% -> 4% of each run, Pallas kernels for 0% -> 0%
where the time goes in v1:
time: 249 us
  waiting for transfers between devices  149 us (60%)
  blocking collectives  29 us (12%)
  matrix products  25.3 us (10%)
  local copies, waits for them, and re-layouts  18 us (7%)
  between operations  14.1 us (6%)
  starting transfers between devices  10.8 us (4%)
  other arithmetic  2.85 us (1%)
    all_to_all x1, waiting for transfers between devices, body(): lax.all_to_all(parts, 'replica', split_axis=0, concat_axis=0, tiled=True)  70.7 us
    all_gather x1, waiting for transfers between devices, body(): update = lax.all_gather(own, 'replica', axis=1, tiled=True)  51.7 us
    all_to_all x1, blocking collectives, body(): lax.all_to_all(by_rows, 'shard', split_axis=0, concat_axis=0, tiled=True)  29 us
    all_to_all x1, waiting for transfers between devices, body(): lax.all_to_all(outgoing, 'shard', split_axis=0, concat_axis=0, tiled=True)  26.3 us
    unnamed x10, local copies, waits for them, and re-layouts  9.41 us
    all_to_all x1, starting transfers between devices, body(): lax.all_to_all(parts, 'replica', split_axis=0, concat_axis=0, tiled=True)  6.45 us
    dot_general x1, matrix products, body(): left_gram = jnp.einsum('tab,tcb->tac', g, g, **f32)  6.34 us
  transfers between devices with their start and end apart: 3, of which 3 were waited for; matrix products, arithmetic and copies ran while one was open for 4% of the time, Pallas kernels for 0%

profile of v1, /device:TPU:0, one launch (start us, length us, event | category | flops | bytes accessed | tf_op | source)
XLA Modules:
  0.0 248.8 jit_solution(16011962881070445816)
XLA Ops:
  7.2 0.0 copy-start
  7.2 4.8 %copy.42 = bf16[1,256,6144]{1,2,0:T(8,128)(2,1)} copy(bf16[1,256,6144]{2,1,0:T(8,128)(2,1)} %param.6) | data formatting | bytes 6291456 | tf_op args[0]
  11.9 6.4 %all-to-all-start = ((bf16[4,3,256,512]{2,3,1,0:T(8,128)(2,1)}), bf16[4,3,256,512]{2,3,1,0:T(8,128)(2,1)}, u32[]{:S(2)}, u32[]{:S(2)}) async-start(bf16[4,3,256,512]{2,3,1,0:T(8,128)(2,1)} %bitcast.43), calls=%async_computation | async-start | bytes 6291456 | tf_op jit(solution)/shard_map/all_to_all | solution.py:21
  18.4 0.0 copy-done.3
  18.4 0.1 fusion.25
  18.5 70.7 %all-to-all-done = bf16[4,3,256,512]{2,3,1,0:T(8,128)(2,1)} async-done(((bf16[4,3,256,512]{2,3,1,0:T(8,128)(2,1)}), bf16[4,3,256,512]{2,3,1,0:T(8,128)(2,1)}, u32[]{:S(2)}, u32[]{:S(2)}) %all-to-all-start) | async-done | bytes 3145760 | tf_op jit(solution)/shard_map/all_to_all | solution.py:21
  89.2 2.5 %reduce_sum.12 = bf16[3,256,512]{1,2,0:T(8,128)(2,1)S(1)} reduce(bf16[4,3,256,512]{2,3,1,0:T(8,128)(2,1)} %all-to-all-done, bf16[]{:T(256)} %constant.59.clone.1), dimensions={0}, to_apply=%region_1.2 | reduce | flops 1179648 | bytes 3932162 | tf_op jit(solution)/shard_map/reduce_sum | solution.py:22
  91.7 1.0 copy.43
  92.7 1.2 fusion.21
  93.9 2.0 copy.44
  95.9 4.3 %all-to-all-start.1 = ((bf16[8,256,512]{2,1,0:T(8,128)(2,1)}), bf16[8,256,512]{2,1,0:T(8,128)(2,1)}, u32[]{:S(2)}, u32[]{:S(2)}) async-start(bf16[8,256,512]{2,1,0:T(8,128)(2,1)} %copy.44), calls=%async_computation.1 | async-start | bytes 4194304 | tf_op jit(solution)/shard_map/all_to_all | solution.py:27
  100.2 0.0 all-gather.2.cloned.1.call-start
  100.3 0.1 constant_dynamic-slice_fusion
  100.4 0.2 compare_reduce_fusion
  100.6 26.3 %all-to-all-done.1 = bf16[8,256,512]{2,1,0:T(8,128)(2,1)} async-done(((bf16[8,256,512]{2,1,0:T(8,128)(2,1)}), bf16[8,256,512]{2,1,0:T(8,128)(2,1)}, u32[]{:S(2)}, u32[]{:S(2)}) %all-to-all-start.1) | async-done | bytes 2097184 | tf_op jit(solution)/shard_map/all_to_all | solution.py:27
  126.9 4.6 %fusion.6 = bf16[3,512,512]{2,0,1:T(4,128)(2,1)} fusion(bf16[4,512,512]{2,1,0:T(8,128)(2,1)} %bitcast.6, pred[3,4]{1,0:T(4,128)(4,1)S(1)} %compare_reduce_fusion), kind=kOutput, calls=%fused_computation.8 | convolution fusion | flops 6291456 | bytes 3670028 | tf_op jit(solution)/shard_map/ti,iab->tab/dot_general | solution.py:31
  131.5 2.9 %copy.48 = bf16[3,512,512]{1,2,0:T(8,128)(2,1)S(1)} copy(bf16[3,512,512]{2,0,1:T(4,128)(2,1)} %fusion.6) | data formatting | bytes 3145728 | tf_op jit(solution)/shard_map/ti,iab->tab/dot_general | solution.py:31
  134.4 0.0 copy-done
  134.4 4.4 %convolution_convert_fusion = bf16[3,512,512]{2,1,0:T(8,128)(2,1)} fusion(bf16[1,3,512,512]{3,2,1,0:T(8,128)(2,1)S(1)} %copy-done, bf16[3,512,512]{1,2,0:T(8,128)(2,1)S(1)} %copy.48, bf16[1,3,512,512]{3,2,1,0:T(8,128)(2,1)} %param.10), kind=kOutput, calls=%fused_computation.10 | convolution fusion | flops 1612185600 | bytes 6291456 | tf_op jit(solution)/shard_map/tab,tbc->tac/dot_general | solution.py:38
  138.8 3.5 %fusion.4 = bf16[4,512,512]{2,0,1:T(4,128)(2,1)S(1)} fusion(bf16[3,512,512]{2,1,0:T(8,128)(2,1)} %convolution_convert_fusion, pred[3,4]{1,0:T(4,128)(4,1)S(1)} %compare_reduce_fusion), kind=kOutput, calls=%fused_computation.6 | convolution fusion | flops 6291456 | bytes 3670028 | tf_op jit(solution)/shard_map/ti,tab->iab/dot_general | solution.py:39
  142.2 0.4 copy.54
  142.7 29.0 %all_to_all.15 = bf16[8,256,512]{2,1,0:T(8,128)(2,1)S(1)} all-to-all(bf16[8,256,512]{2,1,0:T(8,128)(2,1)S(1)} %bitcast.44), channel_id=1, replica_groups=mesh['replica'=4,'shard'=8] {'shard'}, dimensions={0} | all-to-all | bytes 4194304 | tf_op jit(solution)/shard_map/all_to_all | solution.py:41
  171.7 2.4 fusion.10
  174.1 2.3 copy.56
  176.4 0.0 all-gather.2.cloned.1.call-update
  176.4 0.0 copy-start.1
  176.5 0.0 copy-start.2
  176.5 6.3 %fusion.1 = f32[1,3,512,512]{3,2,1,0:T(8,128)} fusion(f32[1,3,512,512]{3,2,1,0:T(8,128)} %param.8, bf16[3,512,512]{2,0,1:T(4,128)(2,1)} %fusion.6), kind=kOutput, calls=%fused_computation.3 | convolution fusion | flops 807665664 | bytes 7864320 | tf_op jit(solution)/shard_map/tab,tcb->tac/dot_general | solution.py:33
  182.8 0.0 copy-done.1
  182.8 2.9 %fusion = f32[1,3,512,512]{3,2,1,0:T(8,128)} fusion(f32[1,3,512,512]{3,2,1,0:T(8,128)S(1)} %copy-done.2, bf16[3,512,512]{1,2,0:T(8,128)(2,1)S(1)} %copy.48, bf16[3,512,512]{2,0,1:T(4,128)(2,1)S(1)} %copy-done.1), kind=kOutput, calls=%fused_computation.1 | convolution fusion | flops 807665664 | bytes 9437184 | tf_op jit(solution)/shard_map/tab,tac->tbc/dot_general | solution.py:34
  185.7 51.7 %all-gather.2.cloned.1.call-done = bf16[256,6144]{0,1:T(8,128)(2,1)} async-done(((bf16[256,1536]{0,1:T(8,128)(2,1)}), bf16[256,6144]{0,1:T(8,128)(2,1)}) %all-gather.2.cloned.1.call-update) | async-done | bytes 3145744 | tf_op jit(solution)/shard_map/all_gather | solution.py:43
  237.3 4.6 %copy.57 = bf16[256,6144]{1,0:T(8,128)(2,1)} copy(bf16[256,6144]{0,1:T(8,128)(2,1)} %all-gather.2.cloned.1.call-done) | data formatting | bytes 6291456
  (3 shorter events, 0.0 us)
Async XLA Ops:
  7.2 127.2 %copy-start = (bf16[1,3,512,512]{3,2,1,0:T(8,128)(2,1)S(1)}, bf16[1,3,512,512]{3,2,1,0:T(8,128)(2,1)}, u32[]{:S(2)}) copy-start(bf16[1,3,512,512]{3,2,1,0:T(8,128)(2,1)} %param.11) | copy-start | bytes 4718596
  11.9 6.5 %copy-start.3 = (s32[4,12]{1,0:T(4,128)S(1)}, s32[4,12]{1,0:T(4,128)}, u32[]{:S(2)}) copy-start(s32[4,12]{1,0:T(4,128)} %param.7) | copy-start | bytes 580
  11.9 77.2 %all-to-all-start = ((bf16[4,3,256,512]{2,3,1,0:T(8,128)(2,1)}), bf16[4,3,256,512]{2,3,1,0:T(8,128)(2,1)}, u32[]{:S(2)}, u32[]{:S(2)}) async-start(bf16[4,3,256,512]{2,3,1,0:T(8,128)(2,1)} %bitcast.43), calls=%async_computation | async-start | bytes 6291456 | tf_op jit(solution)/shard_map/all_to_all | solution.py:21
  95.9 31.0 %all-to-all-start.1 = ((bf16[8,256,512]{2,1,0:T(8,128)(2,1)}), bf16[8,256,512]{2,1,0:T(8,128)(2,1)}, u32[]{:S(2)}, u32[]{:S(2)}) async-start(bf16[8,256,512]{2,1,0:T(8,128)(2,1)} %copy.44), calls=%async_computation.1 | async-start | bytes 4194304 | tf_op jit(solution)/shard_map/all_to_all | solution.py:27
  100.2 137.1 %all-gather.2.cloned.1.call-start = ((), (), s32[]{:S(2)}) async-start(), calls=%async_computation.3 | async-start | bytes 3932160 | tf_op jit(solution)/shard_map/all_gather | solution.py:43
  176.4 6.4 %copy-start.1 = (bf16[3,512,512]{2,0,1:T(4,128)(2,1)S(1)}, bf16[3,512,512]{2,0,1:T(4,128)(2,1)}, u32[]{:S(2)}) copy-start(bf16[3,512,512]{2,0,1:T(4,128)(2,1)} %fusion.6) | copy-start | bytes 4718596
  176.5 6.4 %copy-start.2 = (f32[1,3,512,512]{3,2,1,0:T(8,128)S(1)}, f32[1,3,512,512]{3,2,1,0:T(8,128)}, u32[]{:S(2)}) copy-start(f32[1,3,512,512]{3,2,1,0:T(8,128)} %param.9) | copy-start | bytes 9437188
Sparse Core Ops, SparseCore 0:
  176.6 60.7 all-gather.1

commit v2 on v1

--- a/solution.py
+++ b/solution.py
@@ -1,10 +1,14 @@
+import functools
+
 import jax
 import jax.numpy as jnp
 from jax import lax
+from jax.experimental import pallas as pl
+from jax.experimental.pallas import tpu as pltpu
 from jax.sharding import PartitionSpec as P
 
 
-def body(grads, owner_map, factor_left, factor_right, left_roots, right_roots):
+def plain_body(grads, owner_map, factor_left, factor_right, left_roots, right_roots):
     replicas = lax.axis_size("replica")
     shards = lax.axis_size("shard")
     replica_at = lax.axis_index("replica")
@@ -44,8 +48,439 @@
     return new_left[None], new_right[None], update
 
 
+WIRE = jnp.bfloat16
+
+
+def exchange_kernel(
+    replicas,
+    chunks,
+    slot_ref,
+    valid_ref,
+    grads,
+    left_roots,
+    right_roots,
+    update,
+    gathered,
+    right_in,
+    right_out,
+    left_in,
+    left_out,
+    blocks,
+    products,
+    sib_in,
+    half_in,
+    whole_in,
+    rows_out,
+    right_send,
+    right_recv,
+    left_send,
+    left_recv,
+    gather_send,
+    gather_recv,
+    sib_send,
+    sib_recv,
+    plane_send,
+    plane_recv,
+    up_send,
+    up_recv,
+    down_send,
+    down_recv,
+    block_sem,
+    update_sem,
+):
+    z = lax.axis_index("replica")
+    me = lax.axis_index("shard")
+    last = replicas - 1
+    rows = grads.shape[1]
+    half = rows // 2
+    size = left_roots.shape[2]
+    block_rows = blocks.shape[1] // size
+
+    def other(index, bit):
+        return index + bit - 2 * bit * ((index // bit) % 2)
+
+    sib, near_x, near_y = other(me, 1), other(me, 2), other(me, 4)
+    diag = other(near_x, 4)
+
+    def at(piece, start=0, count=rows):
+        return pl.ds(pl.multiple_of(piece * rows + start, half), count)
+
+    def cols(block):
+        return pl.ds(pl.multiple_of(block * size, size), size)
+
+    def remote(src, dst, send, recv, **where):
+        return pltpu.make_async_remote_copy(
+            src_ref=src,
+            dst_ref=dst,
+            send_sem=send,
+            recv_sem=recv,
+            device_id=where,
+            device_id_type=pl.DeviceIdType.MESH,
+        )
+
+    barrier = pltpu.get_barrier_semaphore()
+
+    def greet(**where):
+        pl.semaphore_signal(
+            barrier, inc=1, device_id=where, device_id_type=pl.DeviceIdType.MESH
+        )
+
+    for neighbour in (sib, near_x, near_y):
+        greet(shard=neighbour)
+    pl.when(z > 0)(lambda: greet(replica=z - 1))
+    pl.when(z < last)(lambda: greet(replica=z + 1))
+    ends = (z == 0) | (z == last)
+    pl.when(ends)(lambda: pl.semaphore_wait(barrier, 4))
+    pl.when(jnp.logical_not(ends))(lambda: pl.semaphore_wait(barrier, 5))
+
+    def to_right(k, d):
+        return remote(
+            right_out.at[k, d],
+            right_in.at[k, d],
+            right_send.at[k, d],
+            right_recv.at[k, d],
+            replica=z + 1,
+        )
+
+    def to_left(k, d):
+        return remote(
+            left_out.at[k, d],
+            left_in.at[k, d],
+            left_send.at[k, d],
+            left_recv.at[k, d],
+            replica=z - 1,
+        )
+
+    def own(block):
+        return grads[0, :, cols(block)].astype(jnp.float32)
+
+    def sum_step(k, j):
+        d = last - j
+
+        @pl.when((z < d) & (z == 0))
+        def _():
+            right_out[k, d] = grads[0, :, cols(d * chunks + k)]
+            to_right(k, d).start()
+
+        @pl.when((z < d) & (z > 0))
+        def _():
+            to_right(k, d).wait_recv()
+            total = own(d * chunks + k) + right_in[k, d].astype(jnp.float32)
+            right_out[k, d] = total.astype(WIRE)
+            to_right(k, d).start()
+
+        e = j
+
+        @pl.when((z > e) & (z == last))
+        def _():
+            left_out[k, e] = grads[0, :, cols(e * chunks + k)]
+            to_left(k, e).start()
+
+        @pl.when((z > e) & (z < last))
+        def _():
+            to_left(k, e).wait_recv()
+            total = own(e * chunks + k) + left_in[k, e].astype(jnp.float32)
+            left_out[k, e] = total.astype(WIRE)
+            to_left(k, e).start()
+
+    def sum_end(k):
+        mine = at(me)
+
+        def store(total):
+            blocks[k, mine] = total.astype(jnp.bfloat16)
+
+        @pl.when(z == 0)
+        def _():
+            to_left(k, z).wait_recv()
+            store(own(z * chunks + k) + left_in[k, z].astype(jnp.float32))
+
+        @pl.when(z == last)
+        def _():
+            to_right(k, z).wait_recv()
+            store(own(z * chunks + k) + right_in[k, z].astype(jnp.float32))
+
+        @pl.when((z > 0) & (z < last))
+        def _():
+            to_right(k, z).wait_recv()
+            to_left(k, z).wait_recv()
+            store(
+                own(z * chunks + k)
+                + right_in[k, z].astype(jnp.float32)
+                + left_in[k, z].astype(jnp.float32)
+            )
+
+    def share(k, n, window, to):
+        return remote(
+            blocks.at[k, window],
+            blocks.at[k, window],
+            gather_send.at[k, n],
+            gather_recv.at[k, n],
+            shard=to,
+        )
+
+    def arrived(k, n, window):
+        share(k, n, window, sib).wait_recv()
+
+    def gather_1(k):
+        share(k, 1, at(me), near_x).start()
+        share(k, 2, at(me), near_y).start()
+        share(k, 0, at(me), sib).start()
+
+    def gather_2(k):
+        arrived(k, 1, at(near_x))
+        share(k, 3, at(near_x, 0, half), near_y).start()
+        arrived(k, 2, at(near_y))
+        share(k, 4, at(near_y, half, half), near_x).start()
+        share(k, 5, at(near_x), sib).start()
+        share(k, 6, at(near_y), sib).start()
+
+    def gather_3(k):
+        arrived(k, 3, at(diag, 0, half))
+        arrived(k, 4, at(diag, half, half))
+        share(k, 7, at(diag), sib).start()
+        arrived(k, 0, at(sib))
+        arrived(k, 5, at(other(sib, 2)))
+        arrived(k, 6, at(other(sib, 4)))
+        arrived(k, 7, at(other(other(sib, 2), 4)))
+
+    def keep_blocks(k):
+        return pltpu.make_async_copy(blocks.at[k], gathered.at[k], block_sem.at[k])
+
+    def compute(k):
+        keep_blocks(k).start()
+
+        def one(i, carry):
+            slot = slot_ref[k * block_rows + i]
+            valid = valid_ref[k * block_rows + i]
+            window = pl.ds(pl.multiple_of(i * size, size), size)
+            applied = jnp.dot(
+                left_roots[0, slot], blocks[k, window], preferred_element_type=jnp.float32
+            ).astype(jnp.bfloat16)
+            product = jnp.dot(
+                applied, right_roots[0, slot], preferred_element_type=jnp.float32
+            )
+            products[k, window] = (product * valid).astype(jnp.bfloat16)
+            return carry
+
+        lax.fori_loop(0, block_rows, one, 0)
+
+    sib_pieces = (sib, other(sib, 2), other(sib, 4), other(other(sib, 2), 4))
+    own_pieces = (me, near_x, near_y, diag)
+
+    def to_sib(k, j):
+        return remote(
+            products.at[k, at(sib_pieces[j])],
+            sib_in.at[k, j],
+            sib_send.at[k, j],
+            sib_recv.at[k, j],
+            shard=sib,
+        )
+
+    def in_plane(k, n):
+        source, target, to = (
+            (products.at[k, at(diag, 0, half)], half_in.at[k, 0], near_x),
+            (products.at[k, at(diag, half, half)], half_in.at[k, 1], near_y),
+            (products.at[k, at(near_x)], whole_in.at[k, 0], near_x),
+            (products.at[k, at(near_y)], whole_in.at[k, 1], near_y),
+        )[n]
+        return remote(source, target, plane_send.at[k, n], plane_recv.at[k, n], shard=to)
+
+    def reduce_1(k):
+        for j in (3, 2, 1, 0):
+            to_sib(k, j).start()
+
+    def reduce_2(k):
+        for j in (3, 2, 1, 0):
+            to_sib(k, j).wait_recv()
+            window = at(own_pieces[j])
+            products[k, window] = products[k, window] + sib_in[k, j]
+            if j == 3:
+                in_plane(k, 0).start()
+                in_plane(k, 1).start()
+
+    def reduce_3(k):
+        in_plane(k, 1).wait_recv()
+        window = at(near_x, half, half)
+        products[k, window] = products[k, window] + half_in[k, 1]
+        in_plane(k, 2).start()
+        in_plane(k, 0).wait_recv()
+        window = at(near_y, 0, half)
+        products[k, window] = products[k, window] + half_in[k, 0]
+        in_plane(k, 3).start()
+
+    def go_up(k, origin):
+        block = origin * chunks + k
+        return remote(
+            rows_out.at[block],
+            rows_out.at[block],
+            up_send.at[block],
+            up_recv.at[block],
+            replica=z + 1,
+        )
+
+    def go_down(k, origin):
+        block = origin * chunks + k
+        return remote(
+            rows_out.at[block],
+            rows_out.at[block],
+            down_send.at[block],
+            down_recv.at[block],
+            replica=z - 1,
+        )
+
+    def write(k, origin):
+        block = origin * chunks + k
+        return pltpu.make_async_copy(
+            rows_out.at[block], update.at[:, cols(block)], update_sem.at[block]
+        )
+
+    def reduce_4(k):
+        in_plane(k, 2).wait_recv()
+        in_plane(k, 3).wait_recv()
+        rows_out[z * chunks + k] = products[k, at(me)] + whole_in[k, 0] + whole_in[k, 1]
+        pl.when(z < last)(lambda: go_up(k, z).start())
+        pl.when(z > 0)(lambda: go_down(k, z).start())
+        write(k, z).start()
+
+    def spread(k, hop):
+        @pl.when(z >= hop)
+        def _():
+            go_up(k, z - hop).wait_recv()
+            pl.when(z < last)(lambda: go_up(k, z - hop).start())
+            write(k, z - hop).start()
+
+        @pl.when(z + hop <= last)
+        def _():
+            go_down(k, z + hop).wait_recv()
+            pl.when(z > 0)(lambda: go_down(k, z + hop).start())
+            write(k, z + hop).start()
+
+    steps = [functools.partial(sum_step, j=j) for j in range(last)]
+
+    def finish_sum(k):
+        sum_end(k)
+        gather_1(k)
+
+    def middle(k):
+        gather_3(k)
+        compute(k)
+        reduce_1(k)
+
+    stages = steps[:-1] + [lambda k: (steps[-1](k), finish_sum(k))]
+    stages += [gather_2, middle, reduce_2, reduce_3, reduce_4]
+    stages += [functools.partial(spread, hop=hop) for hop in range(1, last + 1)]
+    for tick in range(len(stages) + last * (chunks - 1)):
+        for k in reversed(range(chunks)):
+            stage = tick - last * k
+            if 0 <= stage < len(stages):
+                stages[stage](k)
+
+    for k in range(chunks):
+        for d in range(replicas):
+            pl.when(z < d)(lambda: to_right(k, d).wait_send())
+            pl.when(z > d)(lambda: to_left(k, d).wait_send())
+            pl.when((z < last) & (z >= d))(lambda: go_up(k, d).wait_send())
+            pl.when((z > 0) & (z <= d))(lambda: go_down(k, d).wait_send())
+            write(k, d).wait()
+        share(k, 0, at(me), sib).wait_send()
+        share(k, 1, at(me), near_x).wait_send()
+        share(k, 2, at(me), near_y).wait_send()
+        share(k, 3, at(near_x, 0, half), near_y).wait_send()
+        share(k, 4, at(near_y, half, half), near_x).wait_send()
+        share(k, 5, at(near_x), sib).wait_send()
+        share(k, 6, at(near_y), sib).wait_send()
+        share(k, 7, at(diag), sib).wait_send()
+        for n in range(4):
+            to_sib(k, n).wait_send()
+            in_plane(k, n).wait_send()
+        keep_blocks(k).wait()
+
+
+def gram_kernel(size, place, valid, block, left, right, new_left, new_right):
+    t = pl.program_id(0)
+    g = block[0]
+    scale = 0.1 / size * valid[t].astype(jnp.float32)
+    f32 = dict(preferred_element_type=jnp.float32)
+    left_gram = lax.dot_general(g, g, (((1,), (1,)), ((), ())), **f32)
+    new_left[0] = 0.9 * left[0] + scale * left_gram
+    right_gram = lax.dot_general(g, g, (((0,), (0,)), ((), ())), **f32)
+    new_right[0] = 0.9 * right[0] + scale * right_gram
+
+
+def line_body(grads, owner_map, factor_left, factor_right, left_roots, right_roots):
+    replicas = lax.axis_size("replica")
+    shards = lax.axis_size("shard")
+    replica_at = lax.axis_index("replica")
+    shard_at = lax.axis_index("shard")
+    rows, columns = grads.shape[1:]
+    capacity, size = factor_left.shape[1:3]
+    block_rows, block_cols = owner_map.shape
+    chunks = block_cols // replicas
+    total_rows = rows * shards
+    group = lax.dynamic_slice_in_dim(owner_map, replica_at * chunks, chunks, 1).T.reshape(-1)
+    mine = group // capacity == shard_at
+    slots = jnp.where(mine, group % capacity, 0)
+    vmem = pl.BlockSpec(memory_space=pltpu.VMEM)
+    smem = pl.BlockSpec(memory_space=pltpu.SMEM)
+    hbm = pl.BlockSpec(memory_space=pl.ANY)
+    dma = pltpu.SemaphoreType.DMA
+    piece = (rows, size)
+    bf16 = jnp.bfloat16
+    update, gathered = pl.pallas_call(
+        functools.partial(exchange_kernel, replicas, chunks),
+        out_shape=(
+            jax.ShapeDtypeStruct((rows, columns), bf16),
+            jax.ShapeDtypeStruct((chunks, total_rows, size), bf16),
+        ),
+        in_specs=[smem, smem, vmem, vmem, vmem],
+        out_specs=(hbm, hbm),
+        scratch_shapes=[pltpu.VMEM((chunks, replicas) + piece, WIRE)] * 4
+        + [pltpu.VMEM((chunks, total_rows, size), bf16)] * 2
+        + [
+            pltpu.VMEM((chunks, 4) + piece, bf16),
+            pltpu.VMEM((chunks, 2, rows // 2, size), bf16),
+            pltpu.VMEM((chunks, 2) + piece, bf16),
+            pltpu.VMEM((block_cols,) + piece, bf16),
+        ]
+        + [dma((chunks, replicas))] * 4
+        + [dma((chunks, 8))] * 2
+        + [dma((chunks, 4))] * 4
+        + [dma((block_cols,))] * 4
+        + [dma((chunks,)), dma((block_cols,))],
+        compiler_params=pltpu.CompilerParams(
+            collective_id=0, has_side_effects=True, vmem_limit_bytes=56 * 2**20
+        ),
+        name="exchange",
+    )(slots, mine.astype(jnp.float32), grads, left_roots, right_roots)
+
+    targets = shard_at * capacity + jnp.arange(capacity, dtype=jnp.int32)
+    hits = group[None, :] == targets[:, None]
+    place = jnp.sum(jnp.where(hits, jnp.arange(group.shape[0], dtype=jnp.int32), 0), axis=1)
+    valid = jnp.any(hits, axis=1).astype(jnp.int32)
+    square = pl.BlockSpec((1, size, size), lambda t, place, valid: (t, 0, 0))
+    chosen = pl.BlockSpec(
+        (1, size, size),
+        lambda t, place, valid: (place[t] // block_rows, place[t] % block_rows, 0),
+    )
+    factor = jax.ShapeDtypeStruct(factor_left.shape[1:], jnp.float32)
+    new_left, new_right = pl.pallas_call(
+        functools.partial(gram_kernel, size),
+        out_shape=(factor, factor),
+        grid_spec=pltpu.PrefetchScalarGridSpec(
+            num_scalar_prefetch=2,
+            grid=(capacity,),
+            in_specs=[chosen, square, square],
+            out_specs=(square, square),
+        ),
+        compiler_params=pltpu.CompilerParams(vmem_limit_bytes=32 * 2**20),
+        name="grams",
+    )(place, valid, gathered, factor_left[0], factor_right[0])
+    return new_left[None], new_right[None], update
+
+
 def solution(mesh):
     owned = P(("replica", "shard"), None, None, None)
     in_specs = (P("replica", "shard", None), P(), owned, owned, owned, owned)
     out_specs = (owned, owned, P("shard", None))
+    body = line_body if mesh.shape["shard"] == 8 else plain_body
     return jax.shard_map(body, mesh=mesh, in_specs=in_specs, out_specs=out_specs, check_vma=False)

time: 249 us -> 158 us (0.63)
  Pallas kernels: 0 us -> 150 us
  waiting for transfers between devices: 149 us -> 0 us
  blocking collectives: 29 us -> 0 us
  matrix products: 25.3 us -> 0 us
  between operations: 14.1 us -> 0.7 us
  local copies, waits for them, and re-layouts: 18 us -> 5.37 us
  starting transfers between devices: 10.8 us -> 0 us
    pallas_call x0 -> x2, Pallas kernels: none -> 150 us  [the longest x1 146 us: line_body(): pl.pallas_call(functools.partial(exchange_kernel, replicas, chunks), out_...]
    all_to_all x2 -> x0, waiting for transfers between devices: 97 us -> none  [the longest x1 70.7 us: body(): lax.all_to_all(parts, 'replica', split_axis=0, concat_axis=0, tiled=True)]
    all_gather x1 -> x0, waiting for transfers between devices: 51.7 us -> none  [body(): update = lax.all_gather(own, 'replica', axis=1, tiled=True)]
    all_to_all x1 -> x0, blocking collectives: 29 us -> none  [body(): lax.all_to_all(by_rows, 'shard', split_axis=0, concat_axis=0, tiled=True)]
    dot_general x7 -> x0, matrix products: 25.3 us -> none  [the longest x1 6.34 us: body(): left_gram = jnp.einsum('tab,tcb->tac', g, g, **f32)]
    all_to_all x2 -> x0, starting transfers between devices: 10.8 us -> none  [the longest x1 6.45 us: body(): lax.all_to_all(parts, 'replica', split_axis=0, concat_axis=0, tiled=True)]
    dot_general x3 -> x0, local copies, waits for them, and re-layouts: 5.27 us -> none  [the longest x1 2.86 us: body(): g = jnp.einsum('ti,iab->tab', slot_rows, row_blocks)]
    unnamed x10 -> x11, local copies, waits for them, and re-layouts: 9.41 us -> 5.11 us
  transfers between devices with their start and end apart: 3 -> 0, of which waited for: 3 -> 0; matrix products, arithmetic and copies ran while one was open for 4% -> 0% of each run, Pallas kernels for 0% -> 0%
where the time goes in v2:
time: 158 us
  Pallas kernels  150 us (95%)
  local copies, waits for them, and re-layouts  5.37 us (3%)
    pallas_call x1, Pallas kernels, line_body(): pl.pallas_call(functools.partial(exchange_kernel, replicas, chunks), out_...  146 us
    unnamed x11, local copies, waits for them, and re-layouts  5.11 us
    pallas_call x1, Pallas kernels, line_body(): pl.pallas_call(functools.partial(gram_kernel, size), out_shape=(factor, f...  4.13 us

profile of v2, /device:TPU:0, one launch (start us, length us, event | category | flops | bytes accessed | tf_op | source)
XLA Modules:
  0.0 157.8 jit_solution(1617121457049384574)
XLA Ops:
  0.6 0.0 copy-start
  0.7 0.7 copy-done
  1.3 0.1 dynamic-slice_bitcast_fusion
  1.4 0.1 copy.10
  1.5 0.1 eq.23
  1.6 0.2 compare_reduce_fusion
  1.8 0.2 fusion.place
  1.9 0.5 compare_convert_fusion
  2.5 0.5 compare_select_fusion.1.slot_ref
  3.0 0.0 copy-start.2
  3.0 0.0 copy-start.3
  3.0 146.2 %exchange.1 = (bf16[256,6144]{1,0:T(8,128)(2,1)}, bf16[3,2048,512]{2,1,0:T(8,128)(2,1)}) custom-call(s32[12]{0:T(128)} %compare_select_fusion.1.slot_ref, f32[12]{0:T(128)} %get-tuple-element.11.valid_ref, bf16[1,256,6144]{2,1,0:T(8,128)(2,1)} %grads.1, bf16[1,3,512,512]{3,2,1,0:T(8,128)(2,1)} %left_roots.1, bf16[1,3,512,512]{3,2,1,0:T(8,128)(2,1)} %right_roots.1), custom_call_target="tpu_custom_call" | custom-call | tf_op jit(solution)/shard_map/exchange/pallas_call | solution.py:429
  149.2 0.0 copy-done.2
  149.2 0.0 copy-done.3
  149.3 0.0 copy-start.1
  149.3 2.8 %copy-done.1 = bf16[3,2048,512]{2,1,0:T(8,128)(2,1)S(1)} copy-done((bf16[3,2048,512]{2,1,0:T(8,128)(2,1)S(1)}, bf16[3,2048,512]{2,1,0:T(8,128)(2,1)}, u32[]{:S(2)}) %copy-start.1) | copy-done | bytes 6291480
  152.0 0.0 copy-start.4
  152.0 4.1 %grams.1 = (f32[3,512,512]{2,1,0:T(8,128)}, f32[3,512,512]{2,1,0:T(8,128)}) custom-call(s32[3]{0:T(128)S(1)} %fusion.place, s32[3]{0:T(128)S(1)} %convert_element_type.6.valid, bf16[3,2048,512]{2,1,0:T(8,128)(2,1)S(1)} %copy-done.1, f32[3,512,512]{2,1,0:T(8,128)S(1)} %bitcast.6, f32[3,512,512]{2,1,0:T(8,128)S(1)} %bitcast.7), custom_call_target="tpu_custom_call" | custom-call | tf_op jit(solution)/shard_map/grams/pallas_call | solution.py:466
  156.2 0.0 copy-done.4
  156.2 1.7 %copy.12 = bf16[256,6144]{1,0:T(8,128)(2,1)} copy(bf16[256,6144]{1,0:T(8,128)(2,1)S(1)} %copy-done.4) | data formatting | bytes 6291456
  (2 shorter events, 0.0 us)
Async XLA Ops:
  0.6 0.7 copy-start
  3.0 146.2 %copy-start.2 = (f32[1,3,512,512]{3,2,1,0:T(8,128)S(1)}, f32[1,3,512,512]{3,2,1,0:T(8,128)}, u32[]{:S(2)}) copy-start(f32[1,3,512,512]{3,2,1,0:T(8,128)} %param.8) | copy-start | bytes 9437188
  3.0 146.3 %copy-start.3 = (f32[1,3,512,512]{3,2,1,0:T(8,128)S(1)}, f32[1,3,512,512]{3,2,1,0:T(8,128)}, u32[]{:S(2)}) copy-start(f32[1,3,512,512]{3,2,1,0:T(8,128)} %param.9) | copy-start | bytes 9437188
  149.3 2.8 %copy-start.1 = (bf16[3,2048,512]{2,1,0:T(8,128)(2,1)S(1)}, bf16[3,2048,512]{2,1,0:T(8,128)(2,1)}, u32[]{:S(2)}) copy-start(bf16[3,2048,512]{2,1,0:T(8,128)(2,1)} %get-tuple-element.7.block) | copy-start | bytes 18874372
  152.0 4.1 %copy-start.4 = (bf16[256,6144]{1,0:T(8,128)(2,1)S(1)}, bf16[256,6144]{1,0:T(8,128)(2,1)}, u32[]{:S(2)}) copy-start(bf16[256,6144]{1,0:T(8,128)(2,1)} %get-tuple-element.18) | copy-start | bytes 9437188

commit v3 on v2

--- a/solution.py
+++ b/solution.py
@@ -56,11 +56,13 @@
     chunks,
     slot_ref,
     valid_ref,
+    place_ref,
+    held_ref,
     grads,
     left_roots,
     right_roots,
     update,
-    gathered,
+    picked,
     right_in,
     right_out,
     left_in,
@@ -85,7 +87,6 @@
     up_recv,
     down_send,
     down_recv,
-    block_sem,
     update_sem,
 ):
     z = lax.axis_index("replica")
@@ -94,7 +95,7 @@
     rows = grads.shape[1]
     half = rows // 2
     size = left_roots.shape[2]
-    block_rows = blocks.shape[1] // size
+    block_rows = blocks.shape[0] // chunks
 
     def other(index, bit):
         return index + bit - 2 * bit * ((index // bit) % 2)
@@ -104,6 +105,11 @@
 
     def at(piece, start=0, count=rows):
         return pl.ds(pl.multiple_of(piece * rows + start, half), count)
+
+    def spot(piece, start=0, count=rows):
+        per = size // rows
+        first = pl.multiple_of((piece % per) * rows + start, half)
+        return lambda k: (k * block_rows + piece // per, pl.ds(first, count))
 
     def cols(block):
         return pl.ds(pl.multiple_of(block * size, size), size)
@@ -154,40 +160,69 @@
     def own(block):
         return grads[0, :, cols(block)].astype(jnp.float32)
 
+    def raw_right(k, d):
+        right_out[k, d] = grads[0, :, cols(d * chunks + k)]
+        to_right(k, d).start()
+
+    def raw_left(k, d):
+        left_out[k, d] = grads[0, :, cols(d * chunks + k)]
+        to_left(k, d).start()
+
+    def pass_right(k, d):
+        to_right(k, d).wait_recv()
+        total = own(d * chunks + k) + right_in[k, d].astype(jnp.float32)
+        right_out[k, d] = total.astype(WIRE)
+        to_right(k, d).start()
+
+    def pass_left(k, d):
+        to_left(k, d).wait_recv()
+        total = own(d * chunks + k) + left_in[k, d].astype(jnp.float32)
+        left_out[k, d] = total.astype(WIRE)
+        to_left(k, d).start()
+
+    def sum_begin():
+        @pl.when(z == 0)
+        def _():
+            for d in (3, 2, 1):
+                raw_right(0, d)
+
+        @pl.when(z == 3)
+        def _():
+            for d in (0, 1, 2):
+                raw_left(0, d)
+
     def sum_step(k, j):
-        d = last - j
-
-        @pl.when((z < d) & (z == 0))
-        def _():
-            right_out[k, d] = grads[0, :, cols(d * chunks + k)]
-            to_right(k, d).start()
-
-        @pl.when((z < d) & (z > 0))
-        def _():
-            to_right(k, d).wait_recv()
-            total = own(d * chunks + k) + right_in[k, d].astype(jnp.float32)
-            right_out[k, d] = total.astype(WIRE)
-            to_right(k, d).start()
-
-        e = j
-
-        @pl.when((z > e) & (z == last))
-        def _():
-            left_out[k, e] = grads[0, :, cols(e * chunks + k)]
-            to_left(k, e).start()
-
-        @pl.when((z > e) & (z < last))
-        def _():
-            to_left(k, e).wait_recv()
-            total = own(e * chunks + k) + left_in[k, e].astype(jnp.float32)
-            left_out[k, e] = total.astype(WIRE)
-            to_left(k, e).start()
+        @pl.when(z == 0)
+        def _():
+            to_right(k, 3 - j).wait_send()
+            if k + 1 < chunks:
+                raw_right(k + 1, 3 - j)
+
+        @pl.when(z == 3)
+        def _():
+            to_left(k, j).wait_send()
+            if k + 1 < chunks:
+                raw_left(k + 1, j)
+
+        @pl.when(z == 1)
+        def _():
+            if j < 2:
+                pass_right(k, 3 - j)
+            if j == 1:
+                pass_left(k, 0)
+
+        @pl.when(z == 2)
+        def _():
+            if j < 2:
+                pass_left(k, j)
+            if j == 1:
+                pass_right(k, 3)
 
     def sum_end(k):
-        mine = at(me)
+        mine = spot(me)(k)
 
         def store(total):
-            blocks[k, mine] = total.astype(jnp.bfloat16)
+            blocks[mine] = total.astype(jnp.bfloat16)
 
         @pl.when(z == 0)
         def _():
@@ -210,9 +245,10 @@
             )
 
     def share(k, n, window, to):
+        there = blocks.at[window(k)]
         return remote(
-            blocks.at[k, window],
-            blocks.at[k, window],
+            there,
+            there,
             gather_send.at[k, n],
             gather_recv.at[k, n],
             shard=to,
@@ -222,39 +258,39 @@
         share(k, n, window, sib).wait_recv()
 
     def gather_1(k):
-        share(k, 1, at(me), near_x).start()
-        share(k, 2, at(me), near_y).start()
-        share(k, 0, at(me), sib).start()
+        share(k, 1, spot(me), near_x).start()
+        share(k, 2, spot(me), near_y).start()
+        share(k, 0, spot(me), sib).start()
 
     def gather_2(k):
-        arrived(k, 1, at(near_x))
-        share(k, 3, at(near_x, 0, half), near_y).start()
-        arrived(k, 2, at(near_y))
-        share(k, 4, at(near_y, half, half), near_x).start()
-        share(k, 5, at(near_x), sib).start()
-        share(k, 6, at(near_y), sib).start()
+        arrived(k, 1, spot(near_x))
+        share(k, 3, spot(near_x, 0, half), near_y).start()
+        arrived(k, 2, spot(near_y))
+        share(k, 4, spot(near_y, half, half), near_x).start()
+        share(k, 5, spot(near_x), sib).start()
+        share(k, 6, spot(near_y), sib).start()
 
     def gather_3(k):
-        arrived(k, 3, at(diag, 0, half))
-        arrived(k, 4, at(diag, half, half))
-        share(k, 7, at(diag), sib).start()
-        arrived(k, 0, at(sib))
-        arrived(k, 5, at(other(sib, 2)))
-        arrived(k, 6, at(other(sib, 4)))
-        arrived(k, 7, at(other(other(sib, 2), 4)))
-
-    def keep_blocks(k):
-        return pltpu.make_async_copy(blocks.at[k], gathered.at[k], block_sem.at[k])
+        arrived(k, 3, spot(diag, 0, half))
+        arrived(k, 4, spot(diag, half, half))
+        share(k, 7, spot(diag), sib).start()
+        arrived(k, 0, spot(sib))
+        arrived(k, 5, spot(other(sib, 2)))
+        arrived(k, 6, spot(other(sib, 4)))
+        arrived(k, 7, spot(other(other(sib, 2), 4)))
+
+    def pick():
+        for t in range(picked.shape[0]):
+            block = blocks[place_ref[t]]
+            picked[t] = (block.astype(jnp.float32) * held_ref[t]).astype(jnp.bfloat16)
 
     def compute(k):
-        keep_blocks(k).start()
-
         def one(i, carry):
             slot = slot_ref[k * block_rows + i]
             valid = valid_ref[k * block_rows + i]
             window = pl.ds(pl.multiple_of(i * size, size), size)
             applied = jnp.dot(
-                left_roots[0, slot], blocks[k, window], preferred_element_type=jnp.float32
+                left_roots[0, slot], blocks[k * block_rows + i], preferred_element_type=jnp.float32
             ).astype(jnp.bfloat16)
             product = jnp.dot(
                 applied, right_roots[0, slot], preferred_element_type=jnp.float32
@@ -369,37 +405,38 @@
     stages = steps[:-1] + [lambda k: (steps[-1](k), finish_sum(k))]
     stages += [gather_2, middle, reduce_2, reduce_3, reduce_4]
     stages += [functools.partial(spread, hop=hop) for hop in range(1, last + 1)]
+    sum_begin()
     for tick in range(len(stages) + last * (chunks - 1)):
         for k in reversed(range(chunks)):
             stage = tick - last * k
             if 0 <= stage < len(stages):
                 stages[stage](k)
+            if stage == len(stages) - last and k == chunks - 1:
+                pick()
 
     for k in range(chunks):
         for d in range(replicas):
-            pl.when(z < d)(lambda: to_right(k, d).wait_send())
-            pl.when(z > d)(lambda: to_left(k, d).wait_send())
+            pl.when((z > 0) & (z < d))(lambda: to_right(k, d).wait_send())
+            pl.when((z < last) & (z > d))(lambda: to_left(k, d).wait_send())
             pl.when((z < last) & (z >= d))(lambda: go_up(k, d).wait_send())
             pl.when((z > 0) & (z <= d))(lambda: go_down(k, d).wait_send())
             write(k, d).wait()
-        share(k, 0, at(me), sib).wait_send()
-        share(k, 1, at(me), near_x).wait_send()
-        share(k, 2, at(me), near_y).wait_send()
-        share(k, 3, at(near_x, 0, half), near_y).wait_send()
-        share(k, 4, at(near_y, half, half), near_x).wait_send()
-        share(k, 5, at(near_x), sib).wait_send()
-        share(k, 6, at(near_y), sib).wait_send()
-        share(k, 7, at(diag), sib).wait_send()
+        share(k, 0, spot(me), sib).wait_send()
+        share(k, 1, spot(me), near_x).wait_send()
+        share(k, 2, spot(me), near_y).wait_send()
+        share(k, 3, spot(near_x, 0, half), near_y).wait_send()
+        share(k, 4, spot(near_y, half, half), near_x).wait_send()
+        share(k, 5, spot(near_x), sib).wait_send()
+        share(k, 6, spot(near_y), sib).wait_send()
+        share(k, 7, spot(diag), sib).wait_send()
         for n in range(4):
             to_sib(k, n).wait_send()
             in_plane(k, n).wait_send()
-        keep_blocks(k).wait()
-
-
-def gram_kernel(size, place, valid, block, left, right, new_left, new_right):
-    t = pl.program_id(0)
+
+
+def gram_kernel(size, block, left, right, new_left, new_right):
     g = block[0]
-    scale = 0.1 / size * valid[t].astype(jnp.float32)
+    scale = 0.1 / size
     f32 = dict(preferred_element_type=jnp.float32)
     left_gram = lax.dot_general(g, g, (((1,), (1,)), ((), ())), **f32)
     new_left[0] = 0.9 * left[0] + scale * left_gram
@@ -420,22 +457,29 @@
     group = lax.dynamic_slice_in_dim(owner_map, replica_at * chunks, chunks, 1).T.reshape(-1)
     mine = group // capacity == shard_at
     slots = jnp.where(mine, group % capacity, 0)
+    targets = shard_at * capacity + jnp.arange(capacity, dtype=jnp.int32)
+    hits = group[None, :] == targets[:, None]
+    place = jnp.sum(jnp.where(hits, jnp.arange(group.shape[0], dtype=jnp.int32), 0), axis=1)
+    held = jnp.any(hits, axis=1).astype(jnp.float32)
     vmem = pl.BlockSpec(memory_space=pltpu.VMEM)
     smem = pl.BlockSpec(memory_space=pltpu.SMEM)
     hbm = pl.BlockSpec(memory_space=pl.ANY)
     dma = pltpu.SemaphoreType.DMA
     piece = (rows, size)
     bf16 = jnp.bfloat16
-    update, gathered = pl.pallas_call(
+    update, picked = pl.pallas_call(
         functools.partial(exchange_kernel, replicas, chunks),
         out_shape=(
             jax.ShapeDtypeStruct((rows, columns), bf16),
-            jax.ShapeDtypeStruct((chunks, total_rows, size), bf16),
+            jax.ShapeDtypeStruct((capacity, size, size), bf16),
         ),
-        in_specs=[smem, smem, vmem, vmem, vmem],
-        out_specs=(hbm, hbm),
+        in_specs=[smem] * 4 + [vmem] * 3,
+        out_specs=(hbm, vmem),
         scratch_shapes=[pltpu.VMEM((chunks, replicas) + piece, WIRE)] * 4
-        + [pltpu.VMEM((chunks, total_rows, size), bf16)] * 2
+        + [
+            pltpu.VMEM((chunks * block_rows, size, size), bf16),
+            pltpu.VMEM((chunks, total_rows, size), bf16),
+        ]
         + [
             pltpu.VMEM((chunks, 4) + piece, bf16),
             pltpu.VMEM((chunks, 2, rows // 2, size), bf16),
@@ -446,35 +490,24 @@
         + [dma((chunks, 8))] * 2
         + [dma((chunks, 4))] * 4
         + [dma((block_cols,))] * 4
-        + [dma((chunks,)), dma((block_cols,))],
+        + [dma((block_cols,))],
         compiler_params=pltpu.CompilerParams(
             collective_id=0, has_side_effects=True, vmem_limit_bytes=56 * 2**20
         ),
         name="exchange",
-    )(slots, mine.astype(jnp.float32), grads, left_roots, right_roots)
-
-    targets = shard_at * capacity + jnp.arange(capacity, dtype=jnp.int32)
-    hits = group[None, :] == targets[:, None]
-    place = jnp.sum(jnp.where(hits, jnp.arange(group.shape[0], dtype=jnp.int32), 0), axis=1)
-    valid = jnp.any(hits, axis=1).astype(jnp.int32)
-    square = pl.BlockSpec((1, size, size), lambda t, place, valid: (t, 0, 0))
-    chosen = pl.BlockSpec(
-        (1, size, size),
-        lambda t, place, valid: (place[t] // block_rows, place[t] % block_rows, 0),
-    )
+    )(slots, mine.astype(jnp.float32), place, held, grads, left_roots, right_roots)
+
+    square = pl.BlockSpec((1, size, size), lambda t: (t, 0, 0))
     factor = jax.ShapeDtypeStruct(factor_left.shape[1:], jnp.float32)
     new_left, new_right = pl.pallas_call(
         functools.partial(gram_kernel, size),
         out_shape=(factor, factor),
-        grid_spec=pltpu.PrefetchScalarGridSpec(
-            num_scalar_prefetch=2,
-            grid=(capacity,),
-            in_specs=[chosen, square, square],
-            out_specs=(square, square),
-        ),
+        grid=(capacity,),
+        in_specs=[square] * 3,
+        out_specs=(square, square),
         compiler_params=pltpu.CompilerParams(vmem_limit_bytes=32 * 2**20),
         name="grams",
-    )(place, valid, gathered, factor_left[0], factor_right[0])
+    )(picked, factor_left[0], factor_right[0])
     return new_left[None], new_right[None], update
 
 
@@ -482,5 +515,5 @@
     owned = P(("replica", "shard"), None, None, None)
     in_specs = (P("replica", "shard", None), P(), owned, owned, owned, owned)
     out_specs = (owned, owned, P("shard", None))
-    body = line_body if mesh.shape["shard"] == 8 else plain_body
+    body = line_body if dict(mesh.shape) == {"replica": 4, "shard": 8} else plain_body
     return jax.shard_map(body, mesh=mesh, in_specs=in_specs, out_specs=out_specs, check_vma=False)

time: 158 us -> 136 us (0.86)
  Pallas kernels: 150 us -> 128 us
    pallas_call x1, Pallas kernels: 146 us -> 125 us  [line_body(): pl.pallas_call(functools.partial(exchange_kernel, replicas, chunks), out_...]
where the time goes in v3:
time: 136 us
  Pallas kernels  128 us (94%)
  local copies, waits for them, and re-layouts  3.99 us (3%)
  other arithmetic  2.44 us (2%)
    pallas_call x1, Pallas kernels, line_body(): pl.pallas_call(functools.partial(exchange_kernel, replicas, chunks), out_...  125 us
    unnamed x11, local copies, waits for them, and re-layouts  3.74 us
    pallas_call x1, Pallas kernels, line_body(): pl.pallas_call(functools.partial(gram_kernel, size), out_shape=(factor, f...  3.63 us

profile of v3, /device:TPU:0, one launch (start us, length us, event | category | flops | bytes accessed | tf_op | source)
XLA Modules:
  0.0 135.5 jit_solution(1783122781173005054)
XLA Ops:
  0.6 0.0 copy-start
  0.7 0.7 copy-done
  1.3 0.1 dynamic-slice_bitcast_fusion
  1.4 0.1 copy.10
  1.5 0.1 reshape.14
  1.6 0.7 fusion.place_ref
  2.3 0.2 compare_reduce_fusion
  2.5 0.5 convert_element_type.7.held_ref
  3.0 0.5 compare_convert_fusion
  3.5 0.5 compare_select_fusion.1.slot_ref
  4.0 0.0 copy-start.1
  4.0 0.0 copy-start.2
  4.0 124.8 %exchange.1 = (bf16[256,6144]{1,0:T(8,128)(2,1)}, bf16[3,512,512]{2,1,0:T(8,128)(2,1)}) custom-call(s32[12]{0:T(128)} %compare_select_fusion.1.slot_ref, f32[12]{0:T(128)} %get-tuple-element.11.valid_ref, s32[3]{0:T(128)} %fusion.place_ref, f32[3]{0:T(128)} %convert_element_type.7.held_ref, bf16[1,256,6144]{2,1,0:T(8,128)(2,1)} %grads.1, ...), custom_call_target="tpu_custom_call" | custom-call | tf_op jit(solution)/shard_map/exchange/pallas_call | solution.py:470
  128.8 0.0 copy-done.1
  128.8 0.0 copy-done.2
  128.8 0.0 copy-start.3
  128.8 1.4 %copy-done.3 = bf16[3,512,512]{2,1,0:T(8,128)(2,1)S(1)} copy-done((bf16[3,512,512]{2,1,0:T(8,128)(2,1)S(1)}, bf16[3,512,512]{2,1,0:T(8,128)(2,1)}, u32[]{:S(2)}) %copy-start.3) | copy-done | bytes 1572888
  130.2 0.0 copy-start.4
  130.2 3.6 %grams.1 = (f32[3,512,512]{2,1,0:T(8,128)}, f32[3,512,512]{2,1,0:T(8,128)}) custom-call(bf16[3,512,512]{2,1,0:T(8,128)(2,1)S(1)} %copy-done.3, f32[3,512,512]{2,1,0:T(8,128)S(1)} %bitcast.6, f32[3,512,512]{2,1,0:T(8,128)S(1)} %bitcast.7), custom_call_target="tpu_custom_call" | custom-call | tf_op jit(solution)/shard_map/grams/pallas_call | solution.py:502
  133.9 0.0 copy-done.4
  133.9 1.7 %copy.12 = bf16[256,6144]{1,0:T(8,128)(2,1)} copy(bf16[256,6144]{1,0:T(8,128)(2,1)S(1)} %copy-done.4) | data formatting | bytes 6291456
  (1 shorter events, 0.0 us)
Async XLA Ops:
  0.6 0.7 copy-start
  4.0 124.8 %copy-start.1 = (f32[1,3,512,512]{3,2,1,0:T(8,128)S(1)}, f32[1,3,512,512]{3,2,1,0:T(8,128)}, u32[]{:S(2)}) copy-start(f32[1,3,512,512]{3,2,1,0:T(8,128)} %param.8) | copy-start | bytes 9437188
  4.0 124.8 %copy-start.2 = (f32[1,3,512,512]{3,2,1,0:T(8,128)S(1)}, f32[1,3,512,512]{3,2,1,0:T(8,128)}, u32[]{:S(2)}) copy-start(f32[1,3,512,512]{3,2,1,0:T(8,128)} %param.9) | copy-start | bytes 9437188
  128.8 1.4 %copy-start.3 = (bf16[3,512,512]{2,1,0:T(8,128)(2,1)S(1)}, bf16[3,512,512]{2,1,0:T(8,128)(2,1)}, u32[]{:S(2)}) copy-start(bf16[3,512,512]{2,1,0:T(8,128)(2,1)} %get-tuple-element.7.block) | copy-start | bytes 4718596
  130.2 3.6 %copy-start.4 = (bf16[256,6144]{1,0:T(8,128)(2,1)S(1)}, bf16[256,6144]{1,0:T(8,128)(2,1)}, u32[]{:S(2)}) copy-start(bf16[256,6144]{1,0:T(8,128)(2,1)} %get-tuple-element.18) | copy-start | bytes 9437188

commit v4 on v3

--- a/solution.py
+++ b/solution.py
@@ -54,10 +54,7 @@
 def exchange_kernel(
     replicas,
     chunks,
-    slot_ref,
-    valid_ref,
-    place_ref,
-    held_ref,
+    meta_ref,
     grads,
     left_roots,
     right_roots,
@@ -180,29 +177,19 @@
         left_out[k, d] = total.astype(WIRE)
         to_left(k, d).start()
 
-    def sum_begin():
-        @pl.when(z == 0)
-        def _():
-            for d in (3, 2, 1):
-                raw_right(0, d)
-
-        @pl.when(z == 3)
-        def _():
-            for d in (0, 1, 2):
-                raw_left(0, d)
+    def raw(n):
+        k, j = n // 3, n % 3
+        pl.when(z == 0)(lambda: raw_right(k, 3 - j))
+        pl.when(z == 3)(lambda: raw_left(k, j))
 
     def sum_step(k, j):
-        @pl.when(z == 0)
-        def _():
-            to_right(k, 3 - j).wait_send()
-            if k + 1 < chunks:
-                raw_right(k + 1, 3 - j)
-
-        @pl.when(z == 3)
-        def _():
-            to_left(k, j).wait_send()
-            if k + 1 < chunks:
-                raw_left(k + 1, j)
+        pl.when(z == 0)(lambda: to_right(k, 3 - j).wait_send())
+        pl.when(z == 3)(lambda: to_left(k, j).wait_send())
+        n = 3 * k + j
+        ready = (n + 1,) if n < 2 else (3, 4) if n == 2 else (n + 2,)
+        for later in ready:
+            if later < 3 * chunks:
+                raw(later)
 
         @pl.when(z == 1)
         def _():
@@ -281,13 +268,15 @@
 
     def pick():
         for t in range(picked.shape[0]):
-            block = blocks[place_ref[t]]
-            picked[t] = (block.astype(jnp.float32) * held_ref[t]).astype(jnp.bfloat16)
+            place = 2 * chunks * block_rows + t
+            held = meta_ref[place + picked.shape[0]].astype(jnp.float32)
+            block = blocks[meta_ref[place]]
+            picked[t] = (block.astype(jnp.float32) * held).astype(jnp.bfloat16)
 
     def compute(k):
         def one(i, carry):
-            slot = slot_ref[k * block_rows + i]
-            valid = valid_ref[k * block_rows + i]
+            slot = meta_ref[k * block_rows + i]
+            valid = meta_ref[(chunks + k) * block_rows + i].astype(jnp.float32)
             window = pl.ds(pl.multiple_of(i * size, size), size)
             applied = jnp.dot(
                 left_roots[0, slot], blocks[k * block_rows + i], preferred_element_type=jnp.float32
@@ -344,25 +333,15 @@
         products[k, window] = products[k, window] + half_in[k, 0]
         in_plane(k, 3).start()
 
-    def go_up(k, origin):
+    def go_up(k, origin, p):
         block = origin * chunks + k
-        return remote(
-            rows_out.at[block],
-            rows_out.at[block],
-            up_send.at[block],
-            up_recv.at[block],
-            replica=z + 1,
-        )
-
-    def go_down(k, origin):
+        there = rows_out.at[block, pl.ds(p * half, half)]
+        return remote(there, there, up_send.at[block, p], up_recv.at[block, p], replica=z + 1)
+
+    def go_down(k, origin, p):
         block = origin * chunks + k
-        return remote(
-            rows_out.at[block],
-            rows_out.at[block],
-            down_send.at[block],
-            down_recv.at[block],
-            replica=z - 1,
-        )
+        there = rows_out.at[block, pl.ds(p * half, half)]
+        return remote(there, there, down_send.at[block, p], down_recv.at[block, p], replica=z - 1)
 
     def write(k, origin):
         block = origin * chunks + k
@@ -374,22 +353,26 @@
         in_plane(k, 2).wait_recv()
         in_plane(k, 3).wait_recv()
         rows_out[z * chunks + k] = products[k, at(me)] + whole_in[k, 0] + whole_in[k, 1]
-        pl.when(z < last)(lambda: go_up(k, z).start())
-        pl.when(z > 0)(lambda: go_down(k, z).start())
+        for p in range(2):
+            pl.when(z < last)(lambda: go_up(k, z, p).start())
+            pl.when(z > 0)(lambda: go_down(k, z, p).start())
         write(k, z).start()
 
     def spread(k, hop):
-        @pl.when(z >= hop)
-        def _():
-            go_up(k, z - hop).wait_recv()
-            pl.when(z < last)(lambda: go_up(k, z - hop).start())
-            write(k, z - hop).start()
-
-        @pl.when(z + hop <= last)
-        def _():
-            go_down(k, z + hop).wait_recv()
-            pl.when(z > 0)(lambda: go_down(k, z + hop).start())
-            write(k, z + hop).start()
+        for p in range(2):
+
+            @pl.when(z >= hop)
+            def _():
+                go_up(k, z - hop, p).wait_recv()
+                pl.when(z < last)(lambda: go_up(k, z - hop, p).start())
+
+            @pl.when(z + hop <= last)
+            def _():
+                go_down(k, z + hop, p).wait_recv()
+                pl.when(z > 0)(lambda: go_down(k, z + hop, p).start())
+
+        pl.when(z >= hop)(lambda: write(k, z - hop).start())
+        pl.when(z + hop <= last)(lambda: write(k, z + hop).start())
 
     steps = [functools.partial(sum_step, j=j) for j in range(last)]
 
@@ -405,7 +388,7 @@
     stages = steps[:-1] + [lambda k: (steps[-1](k), finish_sum(k))]
     stages += [gather_2, middle, reduce_2, reduce_3, reduce_4]
     stages += [functools.partial(spread, hop=hop) for hop in range(1, last + 1)]
-    sum_begin()
+    raw(0)
     for tick in range(len(stages) + last * (chunks - 1)):
         for k in reversed(range(chunks)):
             stage = tick - last * k
@@ -418,8 +401,9 @@
         for d in range(replicas):
             pl.when((z > 0) & (z < d))(lambda: to_right(k, d).wait_send())
             pl.when((z < last) & (z > d))(lambda: to_left(k, d).wait_send())
-            pl.when((z < last) & (z >= d))(lambda: go_up(k, d).wait_send())
-            pl.when((z > 0) & (z <= d))(lambda: go_down(k, d).wait_send())
+            for p in range(2):
+                pl.when((z < last) & (z >= d))(lambda: go_up(k, d, p).wait_send())
+                pl.when((z > 0) & (z <= d))(lambda: go_down(k, d, p).wait_send())
             write(k, d).wait()
         share(k, 0, spot(me), sib).wait_send()
         share(k, 1, spot(me), near_x).wait_send()
@@ -460,7 +444,8 @@
     targets = shard_at * capacity + jnp.arange(capacity, dtype=jnp.int32)
     hits = group[None, :] == targets[:, None]
     place = jnp.sum(jnp.where(hits, jnp.arange(group.shape[0], dtype=jnp.int32), 0), axis=1)
-    held = jnp.any(hits, axis=1).astype(jnp.float32)
+    held = jnp.any(hits, axis=1).astype(jnp.int32)
+    meta = jnp.concatenate([slots, mine.astype(jnp.int32), place, held])
     vmem = pl.BlockSpec(memory_space=pltpu.VMEM)
     smem = pl.BlockSpec(memory_space=pltpu.SMEM)
     hbm = pl.BlockSpec(memory_space=pl.ANY)
@@ -473,7 +458,7 @@
             jax.ShapeDtypeStruct((rows, columns), bf16),
             jax.ShapeDtypeStruct((capacity, size, size), bf16),
         ),
-        in_specs=[smem] * 4 + [vmem] * 3,
+        in_specs=[smem] + [vmem] * 3,
         out_specs=(hbm, vmem),
         scratch_shapes=[pltpu.VMEM((chunks, replicas) + piece, WIRE)] * 4
         + [
@@ -489,13 +474,13 @@
         + [dma((chunks, replicas))] * 4
         + [dma((chunks, 8))] * 2
         + [dma((chunks, 4))] * 4
-        + [dma((block_cols,))] * 4
+        + [dma((block_cols, 2))] * 4
         + [dma((block_cols,))],
         compiler_params=pltpu.CompilerParams(
             collective_id=0, has_side_effects=True, vmem_limit_bytes=56 * 2**20
         ),
         name="exchange",
-    )(slots, mine.astype(jnp.float32), place, held, grads, left_roots, right_roots)
+    )(meta, grads, left_roots, right_roots)
 
     square = pl.BlockSpec((1, size, size), lambda t: (t, 0, 0))
     factor = jax.ShapeDtypeStruct(factor_left.shape[1:], jnp.float32)

time: 136 us -> 133 us (0.978)
  other arithmetic: 2.44 us -> 0.99 us
    pallas_call x1, Pallas kernels: 125 us -> 123 us  [line_body(): pl.pallas_call(functools.partial(exchange_kernel, replicas, chunks), out_...]
where the time goes in v4:
time: 133 us
  Pallas kernels  127 us (95%)
  local copies, waits for them, and re-layouts  3.99 us (3%)
    pallas_call x1, Pallas kernels, line_body(): pl.pallas_call(functools.partial(exchange_kernel, replicas, chunks), out_...  123 us
    unnamed x11, local copies, waits for them, and re-layouts  3.74 us
    pallas_call x1, Pallas kernels, line_body(): pl.pallas_call(functools.partial(gram_kernel, size), out_shape=(factor, f...  3.63 us

profile of v4, /device:TPU:0, one launch (start us, length us, event | category | flops | bytes accessed | tf_op | source)
XLA Modules:
  0.0 132.6 jit_solution(11881805879829196839)
XLA Ops:
  0.6 0.0 copy-start
  0.7 0.7 copy-done
  1.3 0.1 dynamic-slice_bitcast_fusion
  1.4 0.1 copy.10
  1.5 0.1 reshape.14
  1.6 0.2 fusion
  1.8 0.2 compare_reduce_fusion
  2.0 0.6 pad_add_fusion.meta_ref
  2.6 0.0 copy-start.1
  2.6 0.0 copy-start.2
  2.6 123.3 %exchange.1 = (bf16[256,6144]{1,0:T(8,128)(2,1)}, bf16[3,512,512]{2,1,0:T(8,128)(2,1)}) custom-call(s32[30]{0:T(128)} %pad_add_fusion.meta_ref, bf16[1,256,6144]{2,1,0:T(8,128)(2,1)} %grads.1, bf16[1,3,512,512]{3,2,1,0:T(8,128)(2,1)} %left_roots.1, bf16[1,3,512,512]{3,2,1,0:T(8,128)(2,1)} %right_roots.1), custom_call_target="tpu_custom_call" | custom-call | tf_op jit(solution)/shard_map/exchange/pallas_call | solution.py:455
  125.9 0.0 copy-done.1
  125.9 0.0 copy-done.2
  125.9 0.0 copy-start.3
  125.9 1.4 %copy-done.3 = bf16[3,512,512]{2,1,0:T(8,128)(2,1)S(1)} copy-done((bf16[3,512,512]{2,1,0:T(8,128)(2,1)S(1)}, bf16[3,512,512]{2,1,0:T(8,128)(2,1)}, u32[]{:S(2)}) %copy-start.3) | copy-done | bytes 1572888
  127.3 0.0 copy-start.4
  127.3 3.6 %grams.1 = (f32[3,512,512]{2,1,0:T(8,128)}, f32[3,512,512]{2,1,0:T(8,128)}) custom-call(bf16[3,512,512]{2,1,0:T(8,128)(2,1)S(1)} %copy-done.3, f32[3,512,512]{2,1,0:T(8,128)S(1)} %bitcast.6, f32[3,512,512]{2,1,0:T(8,128)S(1)} %bitcast.7), custom_call_target="tpu_custom_call" | custom-call | tf_op jit(solution)/shard_map/grams/pallas_call | solution.py:487
  131.0 0.0 copy-done.4
  131.0 1.7 %copy.12 = bf16[256,6144]{1,0:T(8,128)(2,1)} copy(bf16[256,6144]{1,0:T(8,128)(2,1)S(1)} %copy-done.4) | data formatting | bytes 6291456
  (4 shorter events, 0.0 us)
Async XLA Ops:
  0.6 0.7 copy-start
  2.6 123.3 %copy-start.1 = (f32[1,3,512,512]{3,2,1,0:T(8,128)S(1)}, f32[1,3,512,512]{3,2,1,0:T(8,128)}, u32[]{:S(2)}) copy-start(f32[1,3,512,512]{3,2,1,0:T(8,128)} %param.8) | copy-start | bytes 9437188
  2.6 123.3 %copy-start.2 = (f32[1,3,512,512]{3,2,1,0:T(8,128)S(1)}, f32[1,3,512,512]{3,2,1,0:T(8,128)}, u32[]{:S(2)}) copy-start(f32[1,3,512,512]{3,2,1,0:T(8,128)} %param.9) | copy-start | bytes 9437188
  125.9 1.4 %copy-start.3 = (bf16[3,512,512]{2,1,0:T(8,128)(2,1)S(1)}, bf16[3,512,512]{2,1,0:T(8,128)(2,1)}, u32[]{:S(2)}) copy-start(bf16[3,512,512]{2,1,0:T(8,128)(2,1)} %get-tuple-element.7.block) | copy-start | bytes 4718596
  127.3 3.6 %copy-start.4 = (bf16[256,6144]{1,0:T(8,128)(2,1)S(1)}, bf16[256,6144]{1,0:T(8,128)(2,1)}, u32[]{:S(2)}) copy-start(bf16[256,6144]{1,0:T(8,128)(2,1)} %get-tuple-element.18) | copy-start | bytes 9437188
